TPU v7x, 32 devices: a whole 2x2x4 slice. The times are simulated.
32 devices in a mesh: vol: 16 (over z, y, core), sub: 2 (over x).
Axes of the slice: x: 2, y: 2, z: 4, core: 2. Of those that a mesh axis runs over, the one named last changes fastest.
Arguments:
- load: float32 [3, 20, 24576], P(None, None, ('vol', 'sub'))
- stiffness: float32 [24576], P(('vol', 'sub')), may hold values from 0.5 to 4
- material: int32 [24576], P(('vol', 'sub')), may hold values from 0 to 1
- stiffness_ref: float32 [2, 60, 60], replicated, as said below
- face_trace: float32 [4, 10, 20], replicated
- adjacency: int32 [4, 24576], P(None, ('vol', 'sub')), may hold values from -1 to 4095, as said below
- penalty: float32 [4, 24576], P(None, ('vol', 'sub')), as said below
- halo_sub: int32 [16384], P(('vol', 'sub')), may hold values from -1 to 3071, as said below
- halo_vol: int32 [16384], P(('vol', 'sub')), may hold values from 0 to 3071, as said below
- fault_send: int32 [4096], P(('vol', 'sub')), may hold values from -1 to 3071, as said below
- fault_target: int32 [4096], P(('vol', 'sub')), may hold values from -1 to 127, as said below
- fault_angles: float32 [2, 4096], P(None, ('vol', 'sub')), may hold values from -3.140625 to 3.140625
- slip_rate: float32 [10, 4096], P(None, ('vol', 'sub')), may hold values from 0.001 to 1
- sigma_eff: float32 [10, 4096], P(None, ('vol', 'sub')), may hold values from 1 to 4
Outputs:
- solution: float32 [3, 20, 24576], P(None, None, ('vol', 'sub'))
- residual: float32 [3, 20, 24576], P(None, None, ('vol', 'sub'))
- slip_next: float32 [10, 4096], P(None, ('vol', 'sub'))
- sigma_next: float32 [10, 4096], P(None, ('vol', 'sub'))
Inputs may be any that keep to these rules, and one draw needn't show every extreme that they name: `adjacency`: A face end paired inside its partition gets the partner's code f * 768 + e; a shared one gets 4 * 768 plus its position among the received columns; -1 is a domain boundary. Pairing is symmetric. `penalty`: paired face ends carry equal weights. `halo_sub`: local face-end codes, distinct within a partition; the block for the partition itself is all -1. `halo_vol`: local face-end codes, distinct within a partition and from those of halo_sub. `fault_send`: each block of 64 slots holds its live codes first, then -1; some partition fills every block in each vol row. Every live code's partner lies in the same partition. `fault_target`: live exactly where fault_send is; the live targets of one grid cell are distinct. `stiffness_ref`: symmetric and diagonally dominant with positive diagonal.
All inputs are finite; a program needn't handle non-finite values.
Results may differ from a plain program's by a relative error of at most 0.0065.
Values sent between devices are 32-bit elements; how exact they have to be, the bound alone decides.
A program may use at most 64 MiB of HBM per device.

v0:
```python
import jax
import jax.numpy as jnp
from jax import lax
from jax.sharding import PartitionSpec as P

ITERS = 2


HIGHEST = lax.Precision.HIGHEST
FRICTION = 0.4
SIGMA_BACK = 3.0
RATE_LENGTH = 0.5
SPEED_REF = 0.2
RATE_DAMP = 0.5
SHEAR_SOFT = 0.01


def with_halo(shard, sides, width):
    for axis, dim in sides:
        peers, length = (lax.axis_size(axis), shard.shape[dim])
        up = [(i, (i + 1) % peers) for i in range(peers - 1)]
        down = [(j, i) for i, j in up]
        last = lax.slice_in_dim(shard, length - width, length, axis=dim)
        leading = lax.slice_in_dim(shard, 0, width, axis=dim)
        before = lax.ppermute(last, axis, up)
        after = lax.ppermute(leading, axis, down)
        shard = jnp.concatenate([before, shard, after], axis=dim)
    return shard


def face_values(nodal_field, face_trace):
    comps, nodes, elems = nodal_field.shape
    faces, face_nodes = (face_trace.shape[0], face_trace.shape[1])
    traced = jnp.einsum("fij,cje->cife", face_trace, nodal_field, precision=HIGHEST)
    return traced.reshape(comps * face_nodes, faces * elems)


def pick_columns(source, codes):
    taken = jnp.take(source, jnp.maximum(codes, 0), axis=1)
    return jnp.where(codes[None, :] >= 0, taken, jnp.zeros_like(taken))


def penalty_flux(traces, remote_cols, adjacency, penalty):
    extended = jnp.concatenate([traces, remote_cols], axis=1)
    nearby = pick_columns(extended, adjacency)
    return penalty[None, :] * (traces - nearby)


def apply_local(
    nodal_field,
    traces,
    remote_cols,
    adjacency,
    penalty,
    stiffness,
    material,
    stiffness_ref,
    face_trace,
):
    comps, nodes, elems = nodal_field.shape
    faces, face_nodes = (face_trace.shape[0], face_trace.shape[1])
    flux_term = penalty_flux(traces, remote_cols, adjacency, penalty).reshape(
        comps, face_nodes, faces, elems
    )
    face_part = jnp.einsum("fij,cife->cje", face_trace, flux_term, precision=HIGHEST)
    flat_field = nodal_field.reshape(comps * nodes, elems)
    both_kinds = jnp.einsum("mab,be->mae", stiffness_ref, flat_field, precision=HIGHEST)
    volume_part = (
        jnp.where(material[None, :] == 1, both_kinds[1], both_kinds[0]) * stiffness[None, :]
    )
    return volume_part.reshape(comps, nodes, elems) + face_part


def jacobi_diag(penalty, stiffness, material, stiffness_ref, face_trace):
    faces, face_nodes, nodes = face_trace.shape
    elems = stiffness.shape[0]
    ref_diag = jnp.diagonal(stiffness_ref, axis1=1, axis2=2)
    volume_part = (
        jnp.where(material[None, :] == 1, ref_diag[1][:, None], ref_diag[0][:, None])
        * stiffness[None, :]
    )
    face_part = jnp.einsum(
        "fij,fe->je", face_trace * face_trace, penalty.reshape(faces, elems), precision=HIGHEST
    )
    comps = ref_diag.shape[1] // nodes
    return volume_part.reshape(comps, nodes, elems) + face_part[None, :, :]


def friction_update(traction, fault_angles, slip_rate, sigma_eff):
    face_nodes = slip_rate.shape[0]
    vectors = traction.reshape(3, face_nodes, -1)
    polar, azimuth = (fault_angles[0], fault_angles[1])
    normal = jnp.stack(
        [jnp.sin(polar) * jnp.cos(azimuth), jnp.sin(polar) * jnp.sin(azimuth), jnp.cos(polar)]
    )
    normal_part = jnp.sum(vectors * normal[:, None, :], axis=0)
    shear_vec = vectors - normal_part[None, :, :] * normal[:, None, :]
    shear_size = jnp.sqrt(jnp.sum(shear_vec * shear_vec, axis=0) + SHEAR_SOFT)
    normal_stress = SIGMA_BACK - normal_part
    sigma_new = sigma_eff - RATE_LENGTH * (slip_rate + SPEED_REF) * (sigma_eff - normal_stress)
    slip_new = jnp.maximum(slip_rate + RATE_DAMP * (shear_size - FRICTION * sigma_new), 0.0)
    return (slip_new, sigma_new)


def local(
    load,
    stiffness,
    material,
    stiffness_ref,
    face_trace,
    adjacency,
    penalty,
    halo_sub,
    halo_vol,
    fault_send,
    fault_target,
    fault_angles,
    slip_rate,
    sigma_eff,
):
    faces = face_trace.shape[0]
    elems = stiffness.shape[0]
    adjacency_flat = adjacency.reshape(faces * elems)
    penalty_flat = penalty.reshape(faces * elems)
    vol_width = halo_vol.shape[0] // 2

    def remote_of(traces):
        sub_send = pick_columns(traces, halo_sub)
        received = lax.all_to_all(sub_send, "sub", split_axis=1, concat_axis=1, tiled=True)
        vol_send = pick_columns(traces, halo_vol)
        rims = with_halo(vol_send, (("vol", 1),), vol_width)
        return jnp.concatenate(
            [received, rims[:, :vol_width], rims[:, rims.shape[1] - vol_width :]], axis=1
        )

    def global_total(value):
        return lax.psum(value, ("vol", "sub"))

    precond = jacobi_diag(penalty_flat, stiffness, material, stiffness_ref, face_trace)
    solution = jnp.zeros_like(load)
    residual = load
    scaled = residual / precond
    search = scaled
    resid_dot = global_total(jnp.sum(residual * scaled))
    for sweep_idx in range(ITERS):
        operator_traces = face_values(search, face_trace)
        image_vec = apply_local(
            search,
            operator_traces,
            remote_of(operator_traces),
            adjacency_flat,
            penalty_flat,
            stiffness,
            material,
            stiffness_ref,
            face_trace,
        )
        step_len = resid_dot / global_total(jnp.sum(search * image_vec))
        solution = solution + step_len * search
        residual = residual - step_len * image_vec
        if sweep_idx + 1 < ITERS:
            scaled = residual / precond
            resid_new = global_total(jnp.sum(residual * scaled))
            search = scaled + resid_new / resid_dot * search
            resid_dot = resid_new
    traces = face_values(solution, face_trace)
    flux_all = penalty_flux(traces, remote_of(traces), adjacency_flat, penalty_flat)
    traction_send = pick_columns(flux_all, fault_send)
    got_traction, got_target = (
        lax.all_to_all(traction_send, "sub", split_axis=1, concat_axis=1, tiled=True),
        lax.all_to_all(fault_target.reshape(1, -1), "sub", split_axis=1, concat_axis=1, tiled=True),
    )
    slot_count = traction_send.shape[1]
    onehot = (got_target[0][:, None] == jnp.arange(slot_count, dtype=jnp.int32)[None, :]).astype(
        jnp.float32
    )
    traction = jnp.dot(got_traction, onehot, precision=HIGHEST, preferred_element_type=jnp.float32)
    slip_new, sigma_new = friction_update(traction, fault_angles, slip_rate, sigma_eff)
    return (solution, residual, slip_new, sigma_new)


def solution(mesh):
    return jax.shard_map(
        local,
        mesh=mesh,
        in_specs=(
            P(None, None, ("vol", "sub")),
            P(("vol", "sub")),
            P(("vol", "sub")),
            P(),
            P(),
            P(None, ("vol", "sub")),
            P(None, ("vol", "sub")),
            P(("vol", "sub")),
            P(("vol", "sub")),
            P(("vol", "sub")),
            P(("vol", "sub")),
            P(None, ("vol", "sub")),
            P(None, ("vol", "sub")),
            P(None, ("vol", "sub")),
        ),
        out_specs=(
            P(None, None, ("vol", "sub")),
            P(None, None, ("vol", "sub")),
            P(None, ("vol", "sub")),
            P(None, ("vol", "sub")),
        ),
        check_vma=False,
    )
```

profile of v0, /device:TPU:0, one launch (start us, length us, event | category | flops | bytes accessed | tf_op | source)
XLA Modules:
  0.0 252.0 jit_solution(2107396835511967487)
XLA Ops:
  2.1 1.6 copy.177
  9.3 2.5 collective-permute-start
  15.1 3.6 %all-to-all-start = ((f32[30,2,256]{2,0,1:T(8,128)}), f32[30,2,256]{2,0,1:T(8,128)S(1)}, u32[]{:S(2)}, u32[]{:S(2)}) async-start(f32[30,2,256]{2,0,1:T(8,128)} %copy.182), calls=%async_computation | async-start | bytes 131072 | tf_op jit(solution)/shard_map/all_to_all | solution.py:129
  23.0 1.6 pad_maximum_fusion
  24.7 10.8 %gather_fusion.4 = f32[3072,30]{1,0:T(8,128)} fusion(f32[30,4096]{0,1:T(8,128)S(1)} %pad_maximum_fusion, s32[3072]{0:T(1024)S(1)} %fusion.31), kind=kCustom, calls=%fused_computation.1.clone | custom fusion | bytes 749568 | tf_op jit(solution)/shard_map/jit(_take)/gather | solution.py:39
  35.5 1.9 copy.187
  38.9 43.8 %all-reduce = (f32[]{:T(128)}, f32[]{:T(128)}) all-reduce(f32[]{:T(128)} %get-tuple-element.7, f32[]{:T(128)} %get-tuple-element.6), channel_id=1, replica_groups=mesh['vol'=16,'sub'=2] {'vol','sub'}, use_global_device_ids=true, to_apply=%region_2.3 | all-reduce | flops 2 | bytes 16 | tf_op jit(solution)/shard_map/psum | solution.py:137
  85.4 41.2 %psum.30 = f32[]{:T(128)} all-reduce(f32[]{:T(128)} %get-tuple-element.14), channel_id=1, replica_groups=mesh['vol'=16,'sub'=2] {'vol','sub'}, use_global_device_ids=true, to_apply=%region_6.9 | all-reduce | flops 1 | bytes 8 | tf_op jit(solution)/shard_map/psum | solution.py:137
  130.4 1.6 gather_fusion.6
  135.0 1.9 collective-permute-start.2
  139.2 3.5 %all-to-all-start.1 = ((f32[30,2,256]{2,0,1:T(8,128)}), f32[30,2,256]{2,0,1:T(8,128)S(1)}, u32[]{:S(2)}, u32[]{:S(2)}) async-start(f32[30,2,256]{2,0,1:T(8,128)} %copy.194), calls=%async_computation.1 | async-start | bytes 131072 | tf_op jit(solution)/shard_map/all_to_all | solution.py:129
  143.9 1.6 squeeze.16
  147.2 1.7 pad_maximum_fusion.1
  148.9 10.8 %gather_fusion.7 = f32[3072,30]{1,0:T(8,128)} fusion(f32[30,4096]{0,1:T(8,128)S(1)} %pad_maximum_fusion.1, s32[3072]{0:T(1024)S(1)} %copy-done.12), kind=kCustom, calls=%fused_computation.7.clone | custom fusion | bytes 749568 | tf_op jit(solution)/shard_map/jit(_take)/gather | solution.py:39
  159.7 1.9 copy.199
  163.2 42.3 %psum.31 = f32[]{:T(128)} all-reduce(f32[]{:T(128)} %get-tuple-element.36), channel_id=1, replica_groups=mesh['vol'=16,'sub'=2] {'vol','sub'}, use_global_device_ids=true, to_apply=%region_8.11 | all-reduce | flops 1 | bytes 8 | tf_op jit(solution)/shard_map/psum | solution.py:137
  215.2 3.5 %all-to-all-start.2 = ((f32[30,2,256]{2,0,1:T(8,128)}), f32[30,2,256]{2,0,1:T(8,128)S(1)}, u32[]{:S(2)}, u32[]{:S(2)}) async-start(f32[30,2,256]{2,0,1:T(8,128)} %copy.205), calls=%async_computation.2 | async-start | bytes 131072 | tf_op jit(solution)/shard_map/all_to_all | solution.py:129
  219.6 3.3 %all-to-all-done.2 = f32[30,2,256]{2,0,1:T(8,128)S(1)} async-done(((f32[30,2,256]{2,0,1:T(8,128)}), f32[30,2,256]{2,0,1:T(8,128)S(1)}, u32[]{:S(2)}, u32[]{:S(2)}) %all-to-all-start.2) | async-done | bytes 61472 | tf_op jit(solution)/shard_map/all_to_all | solution.py:129
  222.9 3.2 %all-to-all-start.4 = ((s32[1,2,64]{2,0,1:T(1,128)}), s32[1,2,64]{2,0,1:T(1,128)S(1)}, u32[]{:S(2)}, u32[]{:S(2)}) async-start(s32[1,2,64]{2,0,1:T(1,128)} %bitcast.41), calls=%async_computation.4 | async-start | bytes 2048 | tf_op jit(solution)/shard_map/all_to_all | solution.py:171
  226.2 1.5 pad_maximum_fusion.2
  227.8 10.8 %gather_fusion.10 = f32[3072,30]{1,0:T(8,128)} fusion(f32[30,4096]{0,1:T(8,128)S(1)} %pad_maximum_fusion.2, s32[3072]{0:T(1024)S(1)} %copy-done.12), kind=kCustom, calls=%fused_computation.8.clone | custom fusion | bytes 749568 | tf_op jit(solution)/shard_map/jit(_take)/gather | solution.py:39
  238.6 1.9 copy.210
  242.6 3.3 %all-to-all-start.3 = ((f32[2,1,1920]{2,1,0:T(1,128)}), f32[2,1,1920]{2,1,0:T(1,128)S(1)}, u32[]{:S(2)}, u32[]{:S(2)}) async-start(f32[2,1,1920]{2,1,0:T(1,128)} %reshape.289), calls=%async_computation.3 | async-start | bytes 30720 | tf_op jit(solution)/shard_map/all_to_all | solution.py:170
  247.1 2.6 %all-to-all-done.3 = f32[2,1,1920]{2,1,0:T(1,128)S(1)} async-done(((f32[2,1,1920]{2,1,0:T(1,128)}), f32[2,1,1920]{2,1,0:T(1,128)S(1)}, u32[]{:S(2)}, u32[]{:S(2)}) %all-to-all-start.3) | async-done | bytes 15392 | tf_op jit(solution)/shard_map/all_to_all | solution.py:170
  (217 shorter events, 43.4 us)
Async XLA Ops:
  5.3 32.4 %copy-start.13 = (pred[768]{0:T(1024)(128)(4,1)}, pred[768]{0:T(1024)(128)(4,1)S(1)}, u32[]{:S(2)}) copy-start(pred[768]{0:T(1024)(128)(4,1)S(1)} %broadcast_compare_fusion.1) | copy-start | bytes 2308
  7.2 11.8 %copy-start = (f32[30,3072]{0,1:T(8,128)}, f32[30,3072]{0,1:T(8,128)S(1)}, u32[]{:S(2)}) copy-start(f32[30,3072]{0,1:T(8,128)S(1)} %copy.185) | copy-start | bytes 1105924
  7.2 11.5 %copy-start.19 = (s32[4,768]{1,0:T(4,128)S(1)}, s32[4,768]{1,0:T(4,128)}, u32[]{:S(2)}) copy-start(s32[4,768]{1,0:T(4,128)} %param.23) | copy-start | bytes 36868
  7.3 11.5 %copy-start.21 = (s32[1024]{0:T(1024)}, s32[1024]{0:T(1024)S(1)}, u32[]{:S(2)}) copy-start(s32[1024]{0:T(1024)S(1)} %pad_clamp_fusion.1) | copy-start | bytes 12292
  7.3 11.7 %copy-start.9 = (f32[2,60,60]{2,0,1:T(2,128)S(1)}, f32[2,60,60]{2,0,1:T(2,128)}, u32[]{:S(2)}) copy-start(f32[2,60,60]{2,0,1:T(2,128)} %param.21) | copy-start | bytes 86404
  9.3 10.9 %copy-start.46 = (f32[2,128]{1,0:T(2,128)S(1)}, f32[2,128]{1,0:T(2,128)}, u32[]{:S(2)}) copy-start(f32[2,128]{1,0:T(2,128)} %param.29) | copy-start | bytes 3076
  9.3 13.7 %collective-permute-start = (f32[30,256]{0,1:T(8,128)}, f32[30,256]{0,1:T(8,128)S(1)}, u32[]{:S(2)}, u32[]{:S(2)}) collective-permute-start(f32[30,256]{0,1:T(8,128)} %get-tuple-element.24), channel_id=1, source_target_pairs={{0,2},{2,4},{4,6},{6,8},{8,10},{10,12},{12,14},{14,16},{16,18},{18... | collective-permute-start | bytes 92168 | tf_op jit(solution)/shard_map/ppermute | solution.py:25
  11.8 11.2 %collective-permute-start.1 = (f32[30,256]{0,1:T(8,128)}, f32[30,256]{0,1:T(8,128)}, u32[]{:S(2)}, u32[]{:S(2)}) collective-permute-start(f32[30,256]{0,1:T(8,128)} %get-tuple-element.25), channel_id=1, source_target_pairs={{2,0},{4,2},{6,4},{8,6},{10,8},{12,10},{14,12},{16,14},{18,16},{20... | collective-permute-start | bytes 92168 | tf_op jit(solution)/shard_map/ppermute | solution.py:26
  15.1 7.7 %all-to-all-start = ((f32[30,2,256]{2,0,1:T(8,128)}), f32[30,2,256]{2,0,1:T(8,128)S(1)}, u32[]{:S(2)}, u32[]{:S(2)}) async-start(f32[30,2,256]{2,0,1:T(8,128)} %copy.182), calls=%async_computation | async-start | bytes 131072 | tf_op jit(solution)/shard_map/all_to_all | solution.py:129
  18.8 18.6 %copy-start.17 = (pred[3072]{0:T(1024)(128)(4,1)}, pred[3072]{0:T(1024)(128)(4,1)S(1)}, u32[]{:S(2)}) copy-start(pred[3072]{0:T(1024)(128)(4,1)S(1)} %compare_and_fusion) | copy-start | bytes 9220
  21.4 16.0 %copy-start.15 = (pred[3072]{0:T(1024)(128)(4,1)}, pred[3072]{0:T(1024)(128)(4,1)S(1)}, u32[]{:S(2)}) copy-start(pred[3072]{0:T(1024)(128)(4,1)S(1)} %ge.48) | copy-start | bytes 9220
  130.4 12.8 %copy-start.2 = (f32[30,3072]{0,1:T(8,128)}, f32[30,3072]{0,1:T(8,128)S(1)}, u32[]{:S(2)}) copy-start(f32[30,3072]{0,1:T(8,128)S(1)} %copy.197) | copy-start | bytes 1105924
  135.0 12.2 %collective-permute-start.2 = (f32[30,256]{0,1:T(8,128)}, f32[30,256]{0,1:T(8,128)}, u32[]{:S(2)}, u32[]{:S(2)}) collective-permute-start(f32[30,256]{0,1:T(8,128)} %get-tuple-element.22), channel_id=1, source_target_pairs={{0,2},{2,4},{4,6},{6,8},{8,10},{10,12},{12,14},{14,16},{16,18},{18... | collective-permute-start | bytes 92168 | tf_op jit(solution)/shard_map/ppermute | solution.py:25
  136.9 10.3 %collective-permute-start.3 = (f32[30,256]{0,1:T(8,128)}, f32[30,256]{0,1:T(8,128)}, u32[]{:S(2)}, u32[]{:S(2)}) collective-permute-start(f32[30,256]{0,1:T(8,128)} %get-tuple-element.23), channel_id=1, source_target_pairs={{2,0},{4,2},{6,4},{8,6},{10,8},{12,10},{14,12},{16,14},{18,16},{20... | collective-permute-start | bytes 92168 | tf_op jit(solution)/shard_map/ppermute | solution.py:26
  139.2 7.8 %all-to-all-start.1 = ((f32[30,2,256]{2,0,1:T(8,128)}), f32[30,2,256]{2,0,1:T(8,128)S(1)}, u32[]{:S(2)}, u32[]{:S(2)}) async-start(f32[30,2,256]{2,0,1:T(8,128)} %copy.194), calls=%async_computation.1 | async-start | bytes 131072 | tf_op jit(solution)/shard_map/all_to_all | solution.py:129
  148.9 12.8 %copy-start.16 = (pred[3072]{0:T(1024)(128)(4,1)S(1)}, pred[3072]{0:T(1024)(128)(4,1)}, u32[]{:S(2)}) copy-start(pred[3072]{0:T(1024)(128)(4,1)} %copy-done.15) | copy-start | bytes 9220
  148.9 12.8 %copy-start.18 = (pred[3072]{0:T(1024)(128)(4,1)S(1)}, pred[3072]{0:T(1024)(128)(4,1)}, u32[]{:S(2)}) copy-start(pred[3072]{0:T(1024)(128)(4,1)} %copy-done.17) | copy-start | bytes 9220
  209.2 17.0 %copy-start.1 = (f32[30,3072]{0,1:T(8,128)}, f32[30,3072]{0,1:T(8,128)S(1)}, u32[]{:S(2)}) copy-start(f32[30,3072]{0,1:T(8,128)S(1)} %copy.208) | copy-start | bytes 1105924
  211.6 14.6 %collective-permute-start.4 = (f32[30,256]{0,1:T(8,128)S(1)}, f32[30,256]{0,1:T(8,128)S(1)}, u32[]{:S(2)}, u32[]{:S(2)}) collective-permute-start(f32[30,256]{0,1:T(8,128)S(1)} %get-tuple-element.20), channel_id=1, source_target_pairs={{0,2},{2,4},{4,6},{6,8},{8,10},{10,12},{12,14},{14,16},{16,18},{18... | collective-permute-start | bytes 92168 | tf_op jit(solution)/shard_map/ppermute | solution.py:25
  212.9 13.3 %collective-permute-start.5 = (f32[30,256]{0,1:T(8,128)S(1)}, f32[30,256]{0,1:T(8,128)S(1)}, u32[]{:S(2)}, u32[]{:S(2)}) collective-permute-start(f32[30,256]{0,1:T(8,128)S(1)} %get-tuple-element.21), channel_id=1, source_target_pairs={{2,0},{4,2},{6,4},{8,6},{10,8},{12,10},{14,12},{16,14},{18,16},{20... | collective-permute-start | bytes 92168 | tf_op jit(solution)/shard_map/ppermute | solution.py:26
  215.2 7.7 %all-to-all-start.2 = ((f32[30,2,256]{2,0,1:T(8,128)}), f32[30,2,256]{2,0,1:T(8,128)S(1)}, u32[]{:S(2)}, u32[]{:S(2)}) async-start(f32[30,2,256]{2,0,1:T(8,128)} %copy.205), calls=%async_computation.2 | async-start | bytes 131072 | tf_op jit(solution)/shard_map/all_to_all | solution.py:129
  222.9 19.7 %all-to-all-start.4 = ((s32[1,2,64]{2,0,1:T(1,128)}), s32[1,2,64]{2,0,1:T(1,128)S(1)}, u32[]{:S(2)}, u32[]{:S(2)}) async-start(s32[1,2,64]{2,0,1:T(1,128)} %bitcast.41), calls=%async_computation.4 | async-start | bytes 2048 | tf_op jit(solution)/shard_map/all_to_all | solution.py:171
  240.5 10.8 %copy-start.28 = (f32[10,128]{1,0:T(8,128)S(1)}, f32[10,128]{1,0:T(8,128)}, u32[]{:S(2)}) copy-start(f32[10,128]{1,0:T(8,128)} %param.30) | copy-start | bytes 15364
  242.6 7.1 %all-to-all-start.3 = ((f32[2,1,1920]{2,1,0:T(1,128)}), f32[2,1,1920]{2,1,0:T(1,128)S(1)}, u32[]{:S(2)}, u32[]{:S(2)}) async-start(f32[2,1,1920]{2,1,0:T(1,128)} %reshape.289), calls=%async_computation.3 | async-start | bytes 30720 | tf_op jit(solution)/shard_map/all_to_all | solution.py:170
  (39 other events, 198.5 us)
where the time goes:
time: 256 us; the launch traced here: 252 us
  blocking collectives  127 us (50%)
  local copies, waits for them, and re-layouts  63.3 us (25%)
  starting transfers between devices  26.7 us (10%)
  other arithmetic  15.7 us (6%)
  waiting for transfers between devices  7.37 us (3%)
  between operations  5.97 us (2%)
  matrix products  5.67 us (2%)
    psum x3, blocking collectives, global_total(): return lax.psum(value, ('vol', 'sub'))  127 us
    gather x14, local copies, waits for them, and re-layouts, pick_columns(): taken = jnp.take(source, jnp.maximum(codes, 0), axis=1)  45.8 us
    all_to_all x3, starting transfers between devices, remote_of(): lax.all_to_all(sub_send, 'sub', split_axis=1, concat_axis=1, tiled=True)  10.7 us
    ppermute x3, starting transfers between devices, with_halo(): before = lax.ppermute(last, axis, up)  5.71 us
  transfers between devices with their start and end apart: 11, of which 4 were waited for; matrix products, arithmetic and copies ran while one was open for 11% of the time, Pallas kernels for 0%

commit v1 on v0

v1 whole, which is shorter than its diff:
```python
import functools

import jax
import jax.numpy as jnp
from jax import lax
from jax.experimental import pallas as pl
from jax.experimental.pallas import tpu as pltpu
from jax.sharding import PartitionSpec as P

FRICTION = 0.4
SIGMA_BACK = 3.0
RATE_LENGTH = 0.5
SPEED_REF = 0.2
RATE_DAMP = 0.5
SHEAR_SOFT = 0.01

HIGHEST = lax.Precision.HIGHEST
MESH = pl.DeviceIdType.MESH
F32, BF16 = jnp.float32, jnp.bfloat16
LANES = 128
ROWS = 32
STRIDE = 24
FIELD = 80


def iota(shape, dim):
    return lax.broadcasted_iota(jnp.int32, shape, dim)


def exact_dot(a, b):
    return lax.dot(a, b, precision=HIGHEST, preferred_element_type=F32)


def split(x):
    high = x.astype(BF16)
    return high, (x - high.astype(F32)).astype(BF16)


def fold_rows(x):
    total = x[0:8]
    for i in range(8, x.shape[0], 8):
        total = total + x[i : i + 8]
    return total


def pick(codes, sources, first, start):
    group = jnp.broadcast_to(lax.shift_right_arithmetic(codes, 7), (8, LANES))
    lane = jnp.broadcast_to(jnp.bitwise_and(codes, LANES - 1), (8, LANES))
    out = [start[8 * r : 8 * r + 8] for r in range(ROWS // 8)]
    for i, source in enumerate(sources):
        hit = group == first + i
        block = source()
        for r in range(ROWS // 8):
            taken = jnp.take_along_axis(
                block[8 * r : 8 * r + 8], lane, axis=1, mode="promise_in_bounds"
            )
            out[r] = jnp.where(hit, taken, out[r])
    return jnp.concatenate(out, axis=0)


def kernel(
    sizes,
    load,
    stiff,
    material,
    stiffness_ref,
    face_trace,
    adjacency,
    penalty,
    halo_sub,
    halo_vol,
    fault_send,
    fault_target,
    angles,
    slip,
    sigma,
    solution_out,
    residual_out,
    slip_out,
    sigma_out,
    field,
    field3,
    ops,
    back3,
    diag_inv,
    trace,
    near,
    flux,
    volume,
    image,
    send_buf,
    recv_buf,
    fault_codes,
    fault_buf,
    fault_recv,
    sums,
    sums_two,
    grid,
    halo_s,
    halo_r,
    fault_s,
    fault_r,
    sum_s,
    sum_r,
):
    n_vol, n_sub, gs, gv, tiles, flat = sizes
    elems = tiles * LANES
    v, s = lax.axis_index("vol"), lax.axis_index("sub")
    n_groups = 4 * tiles
    n_remote = n_sub * gs + 2 * gv

    def sub_peer(d):
        return (v, lax.rem(s + d, n_sub))

    def vol_peer(d):
        return (lax.rem(v + d, n_vol), s)

    def any_peer(d):
        place = lax.rem(v * n_sub + s + d, n_vol * n_sub)
        return (lax.div(place, n_sub), lax.rem(place, n_sub))

    recv_buf[...] = jnp.zeros_like(recv_buf)
    barrier = pltpu.get_barrier_semaphore()
    rounds = [(any_peer, n_vol * n_sub)] if flat else [(sub_peer, n_sub), (vol_peer, n_vol)]
    for peer, count in rounds:

        def greet(d, carry, peer=peer):
            pl.semaphore_signal(barrier, inc=1, device_id=peer(d), device_id_type=MESH)
            return carry

        lax.fori_loop(1, count, greet, 0)

    wide = 256
    col = iota((20, wide), 1)
    inner = lax.rem(col, FIELD)
    node_of = jnp.where((col < 3 * FIELD) & (inner < 3 * STRIDE), lax.rem(inner, STRIDE), -1)
    spread = (node_of == iota((20, wide), 0)).astype(F32)
    row = iota((ROWS, 10), 0)
    lift = ((lax.rem(row, 10) == iota((ROWS, 10), 1)) & (row < 30)).astype(F32)
    same = lax.div(iota((ROWS, wide), 0), 10) == lax.div(
        lax.rem(iota((ROWS, wide), 1), FIELD), STRIDE
    )
    third = iota((1, wide), 1) >= 2 * FIELD

    def store_op(at, value):
        high, low = split(value)
        ops[pl.ds(at, value.shape[0]), :] = jnp.where(
            third, low.astype(F32), high.astype(F32)
        ).astype(BF16)

    faces = []
    for f in range(4):
        full = exact_dot(exact_dot(lift, face_trace[f]), spread)
        faces.append(jnp.where(same, full, 0.0))
    face_all = jnp.concatenate(faces, axis=0)
    store_op(0, face_all)
    back = jnp.transpose(face_all[:, :LANES])[:FIELD]
    back_high, back_low = split(back)
    back3[...] = jnp.concatenate([back_high, back_high, back_low], axis=1)

    a60 = iota((60, wide), 0)
    c60 = iota((60, wide), 1)
    in60 = lax.rem(c60, FIELD)
    place60 = lax.div(in60, STRIDE) * 20 + lax.rem(in60, STRIDE)
    ok60 = (c60 < 3 * FIELD) & (in60 < 3 * STRIDE) & (lax.rem(in60, STRIDE) < 20)
    right = (ok60 & (place60 == a60)).astype(F32)
    rows60 = iota((FIELD, 60), 0)
    left = (
        (rows60 < 3 * STRIDE)
        & (lax.rem(rows60, STRIDE) < 20)
        & (lax.div(rows60, STRIDE) * 20 + lax.rem(rows60, STRIDE) == iota((FIELD, 60), 1))
    ).astype(F32)
    eye = iota((FIELD, wide), 0) == iota((FIELD, wide), 1)
    pad_row = iota((FIELD, 1), 0)
    is_pad = (pad_row >= 3 * STRIDE) | (lax.rem(pad_row, STRIDE) >= 20)
    diag = []
    for m in range(2):
        ref = exact_dot(exact_dot(left, stiffness_ref[m]), right)
        store_op(LANES + m * FIELD, ref)
        entries = jnp.sum(jnp.where(eye, ref, 0.0), axis=1, keepdims=True)
        diag.append(jnp.where(is_pad, 1.0, entries))
    squares = back * back
    weights = []
    lane_face = lax.div(iota((FIELD, LANES), 1), ROWS)
    for f in range(4):
        weights.append(jnp.sum(jnp.where(lane_face == f, squares, 0.0), axis=1, keepdims=True))

    field[...] = jnp.zeros_like(field)
    for c in range(3):
        field[1, c * STRIDE : c * STRIDE + 20, :] = load[c]
    material_one = material[...] == 1
    precond = jnp.where(material_one, diag[1], diag[0]) * stiff[...]
    for f in range(4):
        precond = precond + weights[f] * penalty[f : f + 1, :]
    diag_inv[...] = 1.0 / precond
    field[0] = field[1] * diag_inv[...]

    def make_traces(index, phase):
        high, low = split(field[index])
        field3[...] = jnp.concatenate(
            [high, low, high, jnp.zeros((wide - 3 * FIELD, elems), BF16)], axis=0
        )
        for k in range(tiles):
            trace[phase, k] = lax.dot(
                ops[:LANES, :],
                field3[:, k * LANES : (k + 1) * LANES],
                preferred_element_type=F32,
            )

    def local_sources(ref, phase):
        def source(g):
            return lambda: ref[phase, g % tiles, (g // tiles) * ROWS : (g // tiles + 1) * ROWS, :]

        return [source(g) for g in range(n_groups)]

    nothing = jnp.zeros((ROWS, LANES), F32)

    def halo_copy(phase, i, src, dst, count, device):
        return pltpu.make_async_remote_copy(
            src_ref=send_buf.at[phase, pl.ds(src, count)],
            dst_ref=recv_buf.at[phase, pl.ds(dst, count)],
            send_sem=halo_s.at[phase, i],
            recv_sem=halo_r.at[phase, i],
            device_id=device,
            device_id_type=MESH,
        )

    down = (jnp.maximum(v - 1, 0), s)
    up = (jnp.minimum(v + 1, n_vol - 1), s)

    def halo_copies(phase):
        copies = []
        for d in range(1, n_sub):
            copies.append((None, halo_copy(phase, d - 1, (d - 1) * gs, s * gs, gs, sub_peer(d))))
        low, high = n_sub * gs, n_sub * gs + gv
        copies.append((v > 0, halo_copy(phase, n_sub - 1, low, high, gv, down)))
        copies.append((v < n_vol - 1, halo_copy(phase, n_sub, high, low, gv, up)))
        return copies

    def when(condition, act):
        if condition is None:
            act()
        else:
            pl.when(condition)(act)

    def send_halo(phase, before):
        sources = local_sources(trace, phase)
        copies = halo_copies(phase)
        for part in range(n_sub + 1):
            count = gs if part < n_sub - 1 else gv
            for j in range(count):
                if part < n_sub - 1:
                    peer = lax.rem(s + part + 1, n_sub)
                    codes = halo_sub[pl.ds(peer * gs + j, 1), :]
                    slot = part * gs + j
                else:
                    at = (part - n_sub + 1) * gv + j
                    codes = halo_vol[at : at + 1, :]
                    slot = n_sub * gs + at
                send_buf[phase, slot] = pick(codes, sources, 0, nothing)
            if part == 0:
                before()
            condition, copy = copies[part]
            when(condition, copy.start)

    def wait_halo(phase):
        copies = halo_copies(phase)
        for i in range(n_sub - 1):
            copies[i][1].wait_recv()
        pl.when(v < n_vol - 1)(copies[n_sub - 1][1].wait_recv)
        pl.when(v > 0)(copies[n_sub][1].wait_recv)

    def wait_sent(phase):
        for condition, copy in halo_copies(phase):
            when(condition, copy.wait_send)

    def codes_of(f, k):
        return adjacency[f : f + 1, pl.ds(pl.multiple_of(k * LANES, LANES), LANES)]

    def near_local(phase):
        sources = local_sources(trace, phase)

        def body(k, carry):
            for f in range(4):
                near[k, f * ROWS : (f + 1) * ROWS, :] = pick(codes_of(f, k), sources, 0, nothing)
            return carry

        lax.fori_loop(0, tiles, body, 0)

    def make_flux(phase):
        sources = [lambda g=g: recv_buf[phase, g] for g in range(n_remote)]

        def body(k, carry):
            one, two = carry
            for f in range(4):
                rows = slice(f * ROWS, (f + 1) * ROWS)
                nearby = pick(codes_of(f, k), sources, n_groups, near[k, rows, :])
                weight = penalty[f : f + 1, pl.ds(pl.multiple_of(k * LANES, LANES), LANES)]
                value = weight * (trace[phase, k, rows, :] - nearby)
                flux[phase, k, rows, :] = value
                if phase == 1:
                    one = one + fold_rows(value * trace[0, k, rows, :])
                    two = two + fold_rows(value * trace[1, k, rows, :])
            return one, two

        zero = jnp.zeros((8, LANES), F32)
        return lax.fori_loop(0, tiles, body, (zero, zero))

    def make_volume():
        both = lax.dot(ops[LANES:, :], field3[...], preferred_element_type=F32)
        volume[...] = jnp.where(material_one, both[FIELD:], both[:FIELD]) * stiff[...]

    def finish_image(phase, out, at):
        for k in range(tiles):
            high, low = split(flux[phase, k])
            part = lax.dot(
                back3[...],
                jnp.concatenate([high, low, high], axis=0),
                preferred_element_type=F32,
            )
            cols = slice(k * LANES, (k + 1) * LANES)
            out[at, :, cols] = volume[:, cols] + part

    def dot_tile(a, b):
        rows = fold_rows(a * b)
        total = rows[:, :LANES]
        for k in range(1, tiles):
            total = total + rows[:, k * LANES : (k + 1) * LANES]
        return total

    make_traces(0, 0)
    send_halo(0, lambda: pl.semaphore_wait(barrier, sum(count - 1 for _, count in rounds)))
    near_local(0)
    make_volume()

    cap = LANES // n_sub
    target = jnp.transpose(jnp.broadcast_to(fault_target[...], (LANES, LANES)).astype(F32))
    sent = jnp.transpose(jnp.broadcast_to(fault_send[...], (LANES, LANES)).astype(F32))
    slots = iota((LANES, LANES), 1).astype(F32)
    placed = jnp.where(target == slots, sent, -1.0)
    for t in range(n_sub):
        best = jnp.max(placed[t * cap : (t + 1) * cap], axis=0, keepdims=True)
        fault_codes[t : t + 1, :] = best.astype(jnp.int32)
    polar, azimuth = angles[0:1, :], angles[1:2, :]
    sin_polar = jnp.sin(polar)
    normal = [sin_polar * jnp.cos(azimuth), sin_polar * jnp.sin(azimuth), jnp.cos(polar)]

    wait_halo(0)
    make_flux(0)
    finish_image(0, field, 2)
    field[3] = field[2] * diag_inv[...]

    make_traces(3, 1)
    send_halo(1, lambda: None)
    near_local(1)
    make_volume()
    early = [
        dot_tile(field[1], field[0]),
        dot_tile(field[0], field[2]),
        dot_tile(field[3], field[2]),
    ]
    p_vol, q_vol = dot_tile(field[0], volume[...]), dot_tile(field[3], volume[...])

    def fault_part(phase):
        sources = local_sources(flux, phase)
        for d in range(n_sub):
            codes = fault_codes[pl.ds(lax.rem(s + d, n_sub), 1), :]
            fault_buf[d, phase] = pick(codes, sources, 0, nothing)

    fault_part(0)
    wait_halo(1)
    p_flux, q_flux = make_flux(1)

    parts = [*early, p_vol + p_flux, q_vol + q_flux]
    parts = [jnp.sum(x, axis=0, keepdims=True) for x in parts]
    tile = jnp.concatenate([*parts, jnp.zeros((3, LANES), F32)], axis=0)

    def start_sums(buf, at, peer, count):
        def body(d, carry):
            pltpu.make_async_remote_copy(
                src_ref=buf.at[0],
                dst_ref=buf.at[d],
                send_sem=sum_s.at[at],
                recv_sem=sum_r.at[at],
                device_id=peer(d),
                device_id_type=MESH,
            ).start()
            return carry

        lax.fori_loop(1, count, body, 0)

    def whole(buf, sem, at, count):
        view = buf.at[pl.ds(1, count - 1)]
        pltpu.make_async_copy(view, view, sem.at[at]).wait()

    bufs = [sums, sums_two]
    sums[0] = tile
    start_sums(sums, 0, *rounds[0])

    def fault_copy(d):
        return pltpu.make_async_remote_copy(
            src_ref=fault_buf.at[d],
            dst_ref=fault_recv.at[d - 1],
            send_sem=fault_s.at[d - 1],
            recv_sem=fault_r.at[d - 1],
            device_id=sub_peer(d),
            device_id_type=MESH,
        )

    fault_part(1)
    for d in range(1, n_sub):
        fault_copy(d).start()
    finish_image(1, image, 0)
    wait_sent(0)
    wait_sent(1)

    for at, (peer, count) in enumerate(rounds):
        whole(bufs[at], sum_r, at, count)
        total = jnp.sum(bufs[at][0:count], axis=0)
        if at + 1 < len(rounds):
            bufs[at + 1][0] = total
            start_sums(bufs[at + 1], at + 1, *rounds[at + 1])
    total = jnp.sum(total, axis=1, keepdims=True)
    rz, pw, qw, pv, qv = [total[i : i + 1] for i in range(5)]

    step = rz / pw
    rz_new = step * step * qw - rz
    ratio = rz_new / rz
    along = 1.0 + ratio
    curve = along * along * pw - along * step * (pv + qw) + step * step * qv
    step_two = rz_new / curve
    first = step + step_two * along
    second = step * step_two

    answer = first * field[0] - second * field[3]
    left_over = field[1] - first * field[2] + second * image[0]
    for c in range(3):
        solution_out[c] = answer[c * STRIDE : c * STRIDE + 20]
        residual_out[c] = left_over[c * STRIDE : c * STRIDE + 20]

    for d in range(1, n_sub):
        fault_copy(d).wait_recv()
    base, slope = fault_buf[0, 0], fault_buf[0, 1]
    for d in range(1, n_sub):
        base = base + fault_recv[d - 1, 0]
        slope = slope + fault_recv[d - 1, 1]
    grid[...] = first * base - second * slope
    vectors = [grid[c * 10 : c * 10 + 10, :] for c in range(3)]
    normal_part = vectors[0] * normal[0] + vectors[1] * normal[1] + vectors[2] * normal[2]
    shear = [vectors[c] - normal_part * normal[c] for c in range(3)]
    shear_size = jnp.sqrt(
        shear[0] * shear[0] + shear[1] * shear[1] + shear[2] * shear[2] + SHEAR_SOFT
    )
    rate, old = slip[...], sigma[...]
    fresh = old - RATE_LENGTH * (rate + SPEED_REF) * (old - (SIGMA_BACK - normal_part))
    sigma_out[...] = fresh
    slip_out[...] = jnp.maximum(rate + RATE_DAMP * (shear_size - FRICTION * fresh), 0.0)

    for d in range(1, n_sub):
        fault_copy(d).wait_send()
    for at, (peer, count) in enumerate(rounds):
        whole(bufs[at], sum_s, at, count)


def local(
    load,
    stiffness,
    material,
    stiffness_ref,
    face_trace,
    adjacency,
    penalty,
    halo_sub,
    halo_vol,
    fault_send,
    fault_target,
    fault_angles,
    slip_rate,
    sigma_eff,
):
    n_vol, n_sub = lax.axis_size("vol"), lax.axis_size("sub")
    elems = stiffness.shape[0]
    tiles = elems // LANES
    gs = halo_sub.shape[0] // n_sub // LANES
    gv = halo_vol.shape[0] // 2 // LANES
    remote = n_sub * gs + 2 * gv
    flat = n_vol * n_sub <= 64
    sizes = (n_vol, n_sub, gs, gv, tiles, flat)
    counts = (n_vol * n_sub, 1) if flat else (n_sub, n_vol)
    vmem = pl.BlockSpec(memory_space=pltpu.VMEM)
    dma = pltpu.SemaphoreType.DMA
    return pl.pallas_call(
        functools.partial(kernel, sizes),
        out_shape=(
            jax.ShapeDtypeStruct(load.shape, F32),
            jax.ShapeDtypeStruct(load.shape, F32),
            jax.ShapeDtypeStruct(slip_rate.shape, F32),
            jax.ShapeDtypeStruct(sigma_eff.shape, F32),
        ),
        in_specs=[vmem] * 14,
        out_specs=(vmem,) * 4,
        scratch_shapes=[
            pltpu.VMEM((4, FIELD, elems), F32),
            pltpu.VMEM((256, elems), BF16),
            pltpu.VMEM((LANES + 2 * FIELD, 256), BF16),
            pltpu.VMEM((FIELD, 3 * LANES), BF16),
            pltpu.VMEM((FIELD, elems), F32),
            pltpu.VMEM((2, tiles, LANES, LANES), F32),
            pltpu.VMEM((tiles, LANES, LANES), F32),
            pltpu.VMEM((2, tiles, LANES, LANES), F32),
            pltpu.VMEM((FIELD, elems), F32),
            pltpu.VMEM((1, FIELD, elems), F32),
            pltpu.VMEM((2, remote, ROWS, LANES), F32),
            pltpu.VMEM((2, remote, ROWS, LANES), F32),
            pltpu.VMEM((8, LANES), jnp.int32),
            pltpu.VMEM((n_sub, 2, ROWS, LANES), F32),
            pltpu.VMEM((max(n_sub - 1, 1), 2, ROWS, LANES), F32),
            pltpu.VMEM((counts[0], 8, LANES), F32),
            pltpu.VMEM((counts[1], 8, LANES), F32),
            pltpu.VMEM((ROWS, LANES), F32),
            dma((2, n_sub + 1)),
            dma((2, n_sub + 1)),
            dma((n_sub,)),
            dma((n_sub,)),
            dma((2,)),
            dma((2,)),
        ],
        compiler_params=pltpu.CompilerParams(
            collective_id=0, has_side_effects=True, vmem_limit_bytes=32 * 1024 * 1024
        ),
        name="cg_fault",
    )(
        load,
        stiffness.reshape(1, elems),
        material.reshape(1, elems),
        stiffness_ref,
        face_trace,
        adjacency,
        penalty,
        halo_sub.reshape(n_sub * gs, LANES),
        halo_vol.reshape(2 * gv, LANES),
        fault_send.reshape(1, LANES),
        fault_target.reshape(1, LANES),
        fault_angles,
        slip_rate,
        sigma_eff,
    )


def solution(mesh):
    return jax.shard_map(
        local,
        mesh=mesh,
        in_specs=(
            P(None, None, ("vol", "sub")),
            P(("vol", "sub")),
            P(("vol", "sub")),
            P(),
            P(),
            P(None, ("vol", "sub")),
            P(None, ("vol", "sub")),
            P(("vol", "sub")),
            P(("vol", "sub")),
            P(("vol", "sub")),
            P(("vol", "sub")),
            P(None, ("vol", "sub")),
            P(None, ("vol", "sub")),
            P(None, ("vol", "sub")),
        ),
        out_specs=(
            P(None, None, ("vol", "sub")),
            P(None, None, ("vol", "sub")),
            P(None, ("vol", "sub")),
            P(None, ("vol", "sub")),
        ),
        check_vma=False,
    )
```

time: 256 us -> 29.7 us (0.12); the launches traced: 252 us -> 29.3 us
  blocking collectives: 127 us -> 0 us
  local copies, waits for them, and re-layouts: 63.3 us -> 6.35 us
  starting transfers between devices: 26.7 us -> 0 us
  Pallas kernels: 0 us -> 22.2 us
  other arithmetic: 15.7 us -> 0 us
  waiting for transfers between devices: 7.37 us -> 0 us
  matrix products: 5.67 us -> 0 us
  between operations: 5.97 us -> 0.73 us
    psum x3 -> x0, blocking collectives: 127 us -> none  [global_total(): return lax.psum(value, ('vol', 'sub'))]
    gather x15 -> x0, local copies, waits for them, and re-layouts: 46.9 us -> none  [the longest x14 45.8 us: pick_columns(): taken = jnp.take(source, jnp.maximum(codes, 0), axis=1)]
    pallas_call x0 -> x1, Pallas kernels: none -> 22.2 us  [local(): pl.pallas_call(functools.partial(kernel, sizes), out_shape=(jax.ShapeDtyp...]
    all_to_all x5 -> x0, starting transfers between devices: 17.1 us -> none  [the longest x3 10.7 us: remote_of(): lax.all_to_all(sub_send, 'sub', split_axis=1, concat_axis=1, tiled=True)]
    ppermute x6 -> x0, starting transfers between devices: 9.57 us -> none  [the longest x3 5.71 us: with_halo(): before = lax.ppermute(last, axis, up)]
    all_to_all x5 -> x0, waiting for transfers between devices: 7.35 us -> none  [the longest x3 4.79 us: remote_of(): lax.all_to_all(sub_send, 'sub', split_axis=1, concat_axis=1, tiled=True)]
    dot_general x9 -> x0, matrix products: 5.67 us -> none  [the longest x2 2.31 us: apply_local(): jnp.einsum('fij,cife->cje', face_trace, flux_term, precision=HIGHEST)]
    concatenate x4 -> x0, other arithmetic: 4.89 us -> none  [the longest x3 4.88 us: penalty_flux(): extended = jnp.concatenate([traces, remote_cols], axis=1)]
  transfers between devices with their start and end apart: 11 -> 0, of which waited for: 4 -> 0; matrix products, arithmetic and copies ran while one was open for 11% -> 0% of each run, Pallas kernels for 0% -> 0%
where the time goes in v1:
time: 29.7 us; the launch traced here: 29.3 us
  Pallas kernels  22.2 us (75%)
  local copies, waits for them, and re-layouts  6.35 us (21%)
  between operations  0.73 us (2%)
    pallas_call x1, Pallas kernels, local(): pl.pallas_call(functools.partial(kernel, sizes), out_shape=(jax.ShapeDtyp...  22.2 us
    unnamed x28, local copies, waits for them, and re-layouts  4.95 us
    reshape x1, local copies, waits for them, and re-layouts, local(): stiffness.reshape(1, elems)  0.71 us
    reshape x1, local copies, waits for them, and re-layouts, local(): material.reshape(1, elems)  0.69 us

profile of v1, /device:TPU:0, one launch (start us, length us, event | category | flops | bytes accessed | tf_op | source)
XLA Modules:
  0.0 29.3 jit_solution(7624449782140531496)
XLA Ops:
  0.6 0.7 %reshape.26.stiff = f32[1,768]{1,0:T(1,128)S(1)} reshape(f32[768]{0:T(1024)} %param.15) | data formatting | bytes 6144 | tf_op jit(solution)/shard_map/reshape | solution.py:534
  1.3 0.7 %reshape.27.material = s32[1,768]{1,0:T(1,128)S(1)} reshape(s32[768]{0:T(1024)} %param.16) | data formatting | bytes 6144 | tf_op jit(solution)/shard_map/reshape | solution.py:535
  2.0 0.7 %copy.19.face_trace = f32[4,10,20]{2,1,0:T(8,128)S(1)} copy(f32[4,10,20]{2,0,1:T(4,128)} %param.18) | data formatting | bytes 6400 | tf_op args[4]
  2.8 0.0 copy-done.10
  2.8 0.0 copy-start.3
  2.8 0.0 copy-start.4
  2.8 0.0 copy-start.5
  2.8 0.0 copy-start.6
  2.8 0.0 copy-start.7
  2.8 0.0 copy-start.8
  2.9 0.0 copy-start.9
  2.9 0.6 %copy-done.1 = s32[4,768]{1,0:T(4,128)S(1)} copy-done((s32[4,768]{1,0:T(4,128)S(1)}, s32[4,768]{1,0:T(4,128)}, u32[]{:S(2)}) %copy-start.1) | copy-done | bytes 12312
  3.5 0.0 copy-done.2
  3.5 0.0 copy-done.3
  3.5 0.0 copy-done.4
  3.5 0.0 copy-done.6
  3.5 0.0 copy-done.7
  3.6 0.0 copy-done.9
  3.6 0.9 %copy-done = f32[3,20,768]{2,1,0:T(8,128)S(1)} copy-done((f32[3,20,768]{2,1,0:T(8,128)S(1)}, f32[3,20,768]{2,1,0:T(8,128)}, u32[]{:S(2)}) %copy-start) | copy-done | bytes 184344
  4.5 22.2 %cg_fault.1 = (f32[3,20,768]{2,1,0:T(8,128)S(1)}, f32[3,20,768]{2,1,0:T(8,128)S(1)}, f32[10,128]{1,0:T(8,128)S(1)}, f32[10,128]{1,0:T(8,128)S(1)}) custom-call(f32[3,20,768]{2,1,0:T(8,128)S(1)} %copy-done, f32[1,768]{1,0:T(1,128)S(1)} %reshape.26.stiff, s32[1,768]{1,0:T(1,128)S(1)} %reshape.27.material, f32[2,60,60]{2,1,0:T(8,128)S(1)} %copy.18.stiffness_ref, ...), custom_call_target="tpu_custom_call" | custom-call | tf_op jit(solution)/shard_map/cg_fault/pallas_call | solution.py:492
  26.8 0.7 %copy.24 = f32[3,20,768]{2,1,0:T(8,128)} copy(f32[3,20,768]{2,1,0:T(8,128)S(1)} %get-tuple-element.8) | data formatting | bytes 368640
  27.4 0.7 %copy.25 = f32[3,20,768]{2,1,0:T(8,128)} copy(f32[3,20,768]{2,1,0:T(8,128)S(1)} %get-tuple-element.9) | data formatting | bytes 368640
  28.1 0.6 %copy.26 = f32[10,128]{1,0:T(8,128)} copy(f32[10,128]{1,0:T(8,128)S(1)} %get-tuple-element.10) | data formatting | bytes 10240
  28.7 0.6 %copy.27 = f32[10,128]{1,0:T(8,128)} copy(f32[10,128]{1,0:T(8,128)S(1)} %get-tuple-element.11) | data formatting | bytes 10240
  (7 shorter events, 0.0 us)
Async XLA Ops:
  0.6 2.1 %copy-start.10 = (f32[2,60,60]{2,0,1:T(2,128)S(1)}, f32[2,60,60]{2,0,1:T(2,128)}, u32[]{:S(2)}) copy-start(f32[2,60,60]{2,0,1:T(2,128)} %param.17) | copy-start | bytes 86404
  2.8 0.7 %copy-start.1 = (s32[4,768]{1,0:T(4,128)S(1)}, s32[4,768]{1,0:T(4,128)}, u32[]{:S(2)}) copy-start(s32[4,768]{1,0:T(4,128)} %adjacency.1) | copy-start | bytes 36868
  2.8 0.7 %copy-start.2 = (f32[4,768]{1,0:T(4,128)S(1)}, f32[4,768]{1,0:T(4,128)}, u32[]{:S(2)}) copy-start(f32[4,768]{1,0:T(4,128)} %penalty.1) | copy-start | bytes 36868
  2.8 0.7 %copy-start.3 = (f32[10,128]{1,0:T(8,128)S(1)}, f32[10,128]{1,0:T(8,128)}, u32[]{:S(2)}) copy-start(f32[10,128]{1,0:T(8,128)} %slip.1) | copy-start | bytes 15364
  2.8 0.7 %copy-start.4 = (f32[10,128]{1,0:T(8,128)S(1)}, f32[10,128]{1,0:T(8,128)}, u32[]{:S(2)}) copy-start(f32[10,128]{1,0:T(8,128)} %sigma.1) | copy-start | bytes 15364
  2.8 0.7 %copy-start.5 = (s32[512]{0:T(512)S(1)}, s32[512]{0:T(512)}, u32[]{:S(2)}) copy-start(s32[512]{0:T(512)} %param.21) | copy-start | bytes 6148
  2.8 0.7 %copy-start.6 = (s32[512]{0:T(512)S(1)}, s32[512]{0:T(512)}, u32[]{:S(2)}) copy-start(s32[512]{0:T(512)} %param.22) | copy-start | bytes 6148
  2.8 0.7 %copy-start.7 = (f32[2,128]{1,0:T(2,128)S(1)}, f32[2,128]{1,0:T(2,128)}, u32[]{:S(2)}) copy-start(f32[2,128]{1,0:T(2,128)} %angles.1) | copy-start | bytes 3076
  2.8 0.7 %copy-start.8 = (s32[128]{0:T(128)S(1)}, s32[128]{0:T(128)}, u32[]{:S(2)}) copy-start(s32[128]{0:T(128)} %param.23) | copy-start | bytes 1540
  2.9 0.7 %copy-start.9 = (s32[128]{0:T(128)S(1)}, s32[128]{0:T(128)}, u32[]{:S(2)}) copy-start(s32[128]{0:T(128)} %param.24) | copy-start | bytes 1540
  3.6 0.9 %copy-start = (f32[3,20,768]{2,1,0:T(8,128)S(1)}, f32[3,20,768]{2,1,0:T(8,128)}, u32[]{:S(2)}) copy-start(f32[3,20,768]{2,1,0:T(8,128)} %load.1) | copy-start | bytes 552964

commit v2 on v1

--- a/solution.py
+++ b/solution.py
@@ -20,6 +20,8 @@
 LANES = 128
 ROWS = 32
 STRIDE = 24
+PACKED = 16
+LEVELS = 32700.0
 FIELD = 80
 
 
@@ -43,14 +45,33 @@
     return total
 
 
+def pack(block):
+    size = jnp.max(jnp.abs(block), axis=0, keepdims=True)
+    power = jnp.ceil(jnp.log2(jnp.maximum(size, 1e-35)))
+    whole = jnp.floor((block * jnp.exp2(-power)) * LEVELS + 0.5).astype(jnp.int32)
+    low = whole[PACKED:]
+    last = lax.broadcasted_iota(jnp.int32, low.shape, 0) == PACKED - 1
+    low = jnp.where(last, jnp.broadcast_to(power.astype(jnp.int32), low.shape), low)
+    return jnp.bitwise_or(lax.shift_left(whole[:PACKED], 16), jnp.bitwise_and(low, 0xFFFF))
+
+
+def unpack(packed):
+    high = lax.shift_right_arithmetic(packed, 16)
+    low = lax.shift_right_arithmetic(lax.shift_left(packed, 16), 16)
+    unit = jnp.exp2(low[PACKED - 1 : PACKED].astype(F32)) * (1.0 / LEVELS)
+    last = lax.broadcasted_iota(jnp.int32, low.shape, 0) == PACKED - 1
+    low = jnp.where(last, 0, low)
+    return jnp.concatenate([high, low], axis=0).astype(F32) * unit
+
+
 def pick(codes, sources, first, start):
     group = jnp.broadcast_to(lax.shift_right_arithmetic(codes, 7), (8, LANES))
     lane = jnp.broadcast_to(jnp.bitwise_and(codes, LANES - 1), (8, LANES))
-    out = [start[8 * r : 8 * r + 8] for r in range(ROWS // 8)]
+    out = [start[8 * r : 8 * r + 8] for r in range(PACKED // 8)]
     for i, source in enumerate(sources):
         hit = group == first + i
         block = source()
-        for r in range(ROWS // 8):
+        for r in range(PACKED // 8):
             taken = jnp.take_along_axis(
                 block[8 * r : 8 * r + 8], lane, axis=1, mode="promise_in_bounds"
             )
@@ -58,8 +79,38 @@
     return jnp.concatenate(out, axis=0)
 
 
-def kernel(
+def kernel(sizes, *refs):
+    raw, outs, held, (load_sems, *rest) = refs[:14], refs[14:18], refs[18:32], refs[32:]
+    loads = [pltpu.make_async_copy(a, b, load_sems.at[i]) for i, (a, b) in enumerate(zip(raw, held))]
+    first = (3, 4)
+    order = [*first, *(i for i in range(14) if i not in first)]
+    for i in order:
+        loads[i].start()
+
+    def wait_first():
+        for i in first:
+            loads[i].wait()
+
+    def wait_rest():
+        for i in order[len(first) :]:
+            loads[i].wait()
+
+    run(sizes, wait_first, wait_rest, *held, *outs, *rest)
+
+
+def finish(*refs):
+    sems = refs[-1]
+    copies = [pltpu.make_async_copy(refs[i], refs[i + 4], sems.at[i]) for i in range(4)]
+    for copy in copies:
+        copy.start()
+    for copy in copies:
+        copy.wait()
+
+
+def run(
     sizes,
+    wait_first,
+    wait_rest,
     load,
     stiff,
     material,
@@ -84,6 +135,8 @@
     back3,
     diag_inv,
     trace,
+    packed,
+    packed_remote,
     near,
     flux,
     volume,
@@ -130,6 +183,8 @@
 
         lax.fori_loop(1, count, greet, 0)
 
+    wait_first()
+
     wide = 256
     col = iota((20, wide), 1)
     inner = lax.rem(col, FIELD)
@@ -150,7 +205,7 @@
 
     faces = []
     for f in range(4):
-        full = exact_dot(exact_dot(lift, face_trace[f]), spread)
+        full = exact_dot(exact_dot(lift, face_trace[:, f, :]), spread)
         faces.append(jnp.where(same, full, 0.0))
     face_all = jnp.concatenate(faces, axis=0)
     store_op(0, face_all)
@@ -175,7 +230,7 @@
     is_pad = (pad_row >= 3 * STRIDE) | (lax.rem(pad_row, STRIDE) >= 20)
     diag = []
     for m in range(2):
-        ref = exact_dot(exact_dot(left, stiffness_ref[m]), right)
+        ref = exact_dot(exact_dot(left, stiffness_ref[:, m, :]), right)
         store_op(LANES + m * FIELD, ref)
         entries = jnp.sum(jnp.where(eye, ref, 0.0), axis=1, keepdims=True)
         diag.append(jnp.where(is_pad, 1.0, entries))
@@ -185,11 +240,17 @@
     for f in range(4):
         weights.append(jnp.sum(jnp.where(lane_face == f, squares, 0.0), axis=1, keepdims=True))
 
+    wait_rest()
+
+    def as_row(ref):
+        return jnp.concatenate([ref[k : k + 1, :] for k in range(tiles)], axis=1)
+
+    stiff_row = as_row(stiff)
+    material_one = as_row(material) == 1
     field[...] = jnp.zeros_like(field)
     for c in range(3):
         field[1, c * STRIDE : c * STRIDE + 20, :] = load[c]
-    material_one = material[...] == 1
-    precond = jnp.where(material_one, diag[1], diag[0]) * stiff[...]
+    precond = jnp.where(material_one, diag[1], diag[0]) * stiff_row
     for f in range(4):
         precond = precond + weights[f] * penalty[f : f + 1, :]
     diag_inv[...] = 1.0 / precond
@@ -207,13 +268,15 @@
                 preferred_element_type=F32,
             )
 
-    def local_sources(ref, phase):
-        def source(g):
-            return lambda: ref[phase, g % tiles, (g // tiles) * ROWS : (g // tiles + 1) * ROWS, :]
-
-        return [source(g) for g in range(n_groups)]
-
-    nothing = jnp.zeros((ROWS, LANES), F32)
+    def pack_groups(ref, phase, at):
+        for f in range(4):
+            for k in range(tiles):
+                packed[at, f * tiles + k] = pack(ref[phase, k, f * ROWS : (f + 1) * ROWS, :])
+
+    def local_sources(at):
+        return [lambda g=g: packed[at, g] for g in range(n_groups)]
+
+    nothing = jnp.zeros((PACKED, LANES), jnp.int32)
 
     def halo_copy(phase, i, src, dst, count, device):
         return pltpu.make_async_remote_copy(
@@ -244,7 +307,8 @@
             pl.when(condition)(act)
 
     def send_halo(phase, before):
-        sources = local_sources(trace, phase)
+        pack_groups(trace, phase, 0)
+        sources = local_sources(0)
         copies = halo_copies(phase)
         for part in range(n_sub + 1):
             count = gs if part < n_sub - 1 else gv
@@ -257,7 +321,7 @@
                     at = (part - n_sub + 1) * gv + j
                     codes = halo_vol[at : at + 1, :]
                     slot = n_sub * gs + at
-                send_buf[phase, slot] = pick(codes, sources, 0, nothing)
+                send_buf[phase, slot] = unpack(pick(codes, sources, 0, nothing))
             if part == 0:
                 before()
             condition, copy = copies[part]
@@ -275,40 +339,34 @@
             when(condition, copy.wait_send)
 
     def codes_of(f, k):
-        return adjacency[f : f + 1, pl.ds(pl.multiple_of(k * LANES, LANES), LANES)]
-
-    def near_local(phase):
-        sources = local_sources(trace, phase)
-
-        def body(k, carry):
-            for f in range(4):
-                near[k, f * ROWS : (f + 1) * ROWS, :] = pick(codes_of(f, k), sources, 0, nothing)
-            return carry
-
-        lax.fori_loop(0, tiles, body, 0)
+        return adjacency[f : f + 1, k * LANES : (k + 1) * LANES]
+
+    def near_local():
+        sources = local_sources(0)
+        for f in range(4):
+            for k in range(tiles):
+                near[f * tiles + k] = pick(codes_of(f, k), sources, 0, nothing)
 
     def make_flux(phase):
-        sources = [lambda g=g: recv_buf[phase, g] for g in range(n_remote)]
-
-        def body(k, carry):
-            one, two = carry
-            for f in range(4):
-                rows = slice(f * ROWS, (f + 1) * ROWS)
-                nearby = pick(codes_of(f, k), sources, n_groups, near[k, rows, :])
-                weight = penalty[f : f + 1, pl.ds(pl.multiple_of(k * LANES, LANES), LANES)]
-                value = weight * (trace[phase, k, rows, :] - nearby)
+        for g in range(n_remote):
+            packed_remote[g] = pack(recv_buf[phase, g])
+        sources = [lambda g=g: packed_remote[g] for g in range(n_remote)]
+        one = two = jnp.zeros((8, LANES), F32)
+        for f in range(4):
+            rows = slice(f * ROWS, (f + 1) * ROWS)
+            for k in range(tiles):
+                nearby = pick(codes_of(f, k), sources, n_groups, near[f * tiles + k])
+                weight = penalty[f : f + 1, k * LANES : (k + 1) * LANES]
+                value = weight * (trace[phase, k, rows, :] - unpack(nearby))
                 flux[phase, k, rows, :] = value
                 if phase == 1:
                     one = one + fold_rows(value * trace[0, k, rows, :])
                     two = two + fold_rows(value * trace[1, k, rows, :])
-            return one, two
-
-        zero = jnp.zeros((8, LANES), F32)
-        return lax.fori_loop(0, tiles, body, (zero, zero))
+        return one, two
 
     def make_volume():
         both = lax.dot(ops[LANES:, :], field3[...], preferred_element_type=F32)
-        volume[...] = jnp.where(material_one, both[FIELD:], both[:FIELD]) * stiff[...]
+        volume[...] = jnp.where(material_one, both[FIELD:], both[:FIELD]) * stiff_row
 
     def finish_image(phase, out, at):
         for k in range(tiles):
@@ -330,7 +388,7 @@
 
     make_traces(0, 0)
     send_halo(0, lambda: pl.semaphore_wait(barrier, sum(count - 1 for _, count in rounds)))
-    near_local(0)
+    near_local()
     make_volume()
 
     cap = LANES // n_sub
@@ -352,7 +410,7 @@
 
     make_traces(3, 1)
     send_halo(1, lambda: None)
-    near_local(1)
+    near_local()
     make_volume()
     early = [
         dot_tile(field[1], field[0]),
@@ -362,10 +420,11 @@
     p_vol, q_vol = dot_tile(field[0], volume[...]), dot_tile(field[3], volume[...])
 
     def fault_part(phase):
-        sources = local_sources(flux, phase)
+        pack_groups(flux, phase, 1)
+        sources = local_sources(1)
         for d in range(n_sub):
             codes = fault_codes[pl.ds(lax.rem(s + d, n_sub), 1), :]
-            fault_buf[d, phase] = pick(codes, sources, 0, nothing)
+            fault_buf[d, phase] = unpack(pick(codes, sources, 0, nothing))
 
     fault_part(0)
     wait_halo(1)
@@ -484,29 +543,47 @@
     gs = halo_sub.shape[0] // n_sub // LANES
     gv = halo_vol.shape[0] // 2 // LANES
     remote = n_sub * gs + 2 * gv
+    n_groups = 4 * tiles
     flat = n_vol * n_sub <= 64
     sizes = (n_vol, n_sub, gs, gv, tiles, flat)
     counts = (n_vol * n_sub, 1) if flat else (n_sub, n_vol)
     vmem = pl.BlockSpec(memory_space=pltpu.VMEM)
+    anywhere = pl.BlockSpec(memory_space=pl.ANY)
     dma = pltpu.SemaphoreType.DMA
-    return pl.pallas_call(
+    inputs = (
+        load,
+        stiffness.reshape(tiles, LANES),
+        material.reshape(tiles, LANES),
+        jnp.transpose(stiffness_ref, (1, 0, 2)),
+        jnp.transpose(face_trace, (1, 0, 2)),
+        adjacency,
+        penalty,
+        halo_sub.reshape(n_sub * gs, LANES),
+        halo_vol.reshape(2 * gv, LANES),
+        fault_send.reshape(1, LANES),
+        fault_target.reshape(1, LANES),
+        fault_angles,
+        slip_rate,
+        sigma_eff,
+    )
+    shapes = tuple(jax.ShapeDtypeStruct(x.shape, F32) for x in (load, load, slip_rate, sigma_eff))
+    outs = pl.pallas_call(
         functools.partial(kernel, sizes),
-        out_shape=(
-            jax.ShapeDtypeStruct(load.shape, F32),
-            jax.ShapeDtypeStruct(load.shape, F32),
-            jax.ShapeDtypeStruct(slip_rate.shape, F32),
-            jax.ShapeDtypeStruct(sigma_eff.shape, F32),
-        ),
-        in_specs=[vmem] * 14,
+        out_shape=tuple(pltpu.VMEM(x.shape, x.dtype) for x in shapes),
+        in_specs=[pl.BlockSpec(memory_space=pltpu.HBM)] * 14,
         out_specs=(vmem,) * 4,
         scratch_shapes=[
+            *(pltpu.VMEM(x.shape, x.dtype) for x in inputs),
+            dma((14,)),
             pltpu.VMEM((4, FIELD, elems), F32),
             pltpu.VMEM((256, elems), BF16),
             pltpu.VMEM((LANES + 2 * FIELD, 256), BF16),
             pltpu.VMEM((FIELD, 3 * LANES), BF16),
             pltpu.VMEM((FIELD, elems), F32),
             pltpu.VMEM((2, tiles, LANES, LANES), F32),
-            pltpu.VMEM((tiles, LANES, LANES), F32),
+            pltpu.VMEM((2, n_groups, PACKED, LANES), jnp.int32),
+            pltpu.VMEM((remote, PACKED, LANES), jnp.int32),
+            pltpu.VMEM((n_groups, PACKED, LANES), jnp.int32),
             pltpu.VMEM((2, tiles, LANES, LANES), F32),
             pltpu.VMEM((FIELD, elems), F32),
             pltpu.VMEM((1, FIELD, elems), F32),
@@ -525,26 +602,18 @@
             dma((2,)),
             dma((2,)),
         ],
-        compiler_params=pltpu.CompilerParams(
-            collective_id=0, has_side_effects=True, vmem_limit_bytes=32 * 1024 * 1024
-        ),
+        compiler_params=pltpu.CompilerParams(collective_id=0, has_side_effects=True, vmem_limit_bytes=32 * 1024 * 1024),
         name="cg_fault",
-    )(
-        load,
-        stiffness.reshape(1, elems),
-        material.reshape(1, elems),
-        stiffness_ref,
-        face_trace,
-        adjacency,
-        penalty,
-        halo_sub.reshape(n_sub * gs, LANES),
-        halo_vol.reshape(2 * gv, LANES),
-        fault_send.reshape(1, LANES),
-        fault_target.reshape(1, LANES),
-        fault_angles,
-        slip_rate,
-        sigma_eff,
-    )
+    )(*(pltpu.with_memory_space_constraint(x, pltpu.HBM) for x in inputs))
+    return pl.pallas_call(
+        finish,
+        out_shape=shapes,
+        in_specs=[vmem] * 4,
+        out_specs=(anywhere,) * 4,
+        scratch_shapes=[dma((4,))],
+        compiler_params=pltpu.CompilerParams(vmem_limit_bytes=16 * 1024 * 1024),
+        name="finish",
+    )(*(pltpu.with_memory_space_constraint(x, pltpu.VMEM) for x in outs))
 
 
 def solution(mesh):

time: 29.7 us -> 21 us (0.71)
  local copies, waits for them, and re-layouts: 6.35 us -> 0 us
  Pallas kernels: 22.2 us -> 20.2 us
    unnamed x28 -> x0, local copies, waits for them, and re-layouts: 4.95 us -> none
    pallas_call x1 -> x2, Pallas kernels: 22.2 us -> 20.2 us  [the longest x1 19.4 us: local(): pl.pallas_call(functools.partial(kernel, sizes), out_shape=tuple((pltpu.V...]
    reshape x2 -> x0, local copies, waits for them, and re-layouts: 1.4 us -> none  [the longest x1 0.71 us: local(): stiffness.reshape(1, elems)]
where the time goes in v2:
time: 21 us; the launch traced here: 20.8 us
  Pallas kernels  20.2 us (96%)
  between operations  0.64 us (3%)
    pallas_call x1, Pallas kernels, local(): pl.pallas_call(functools.partial(kernel, sizes), out_shape=tuple((pltpu.V...  19.4 us
    pallas_call x1, Pallas kernels, local(): pl.pallas_call(finish, out_shape=shapes, in_specs=[vmem] * 4, out_specs=(...  0.8 us

profile of v2, /device:TPU:0, one launch (start us, length us, event | category | flops | bytes accessed | tf_op | source)
XLA Modules:
  0.0 20.8 jit_solution(10458856096839593726)
XLA Ops:
  0.6 19.4 %cg_fault.1 = (f32[3,20,768]{2,1,0:T(8,128)S(1)}, f32[3,20,768]{2,1,0:T(8,128)S(1)}, f32[10,128]{1,0:T(8,128)S(1)}, f32[10,128]{1,0:T(8,128)S(1)}) custom-call(f32[3,20,768]{2,1,0:T(8,128)} %refs_0_.1, f32[6,128]{1,0:T(8,128)} %bitcast.10, s32[6,128]{1,0:T(8,128)} %bitcast.11, f32[60,2,60]{2,1,0:T(2,128)} %bitcast.8, f32[10,4,20]{2,1,0:T(4,128)} %bitcast.9, ...), custom_call_target="tpu_custom_call" | custom-call | tf_op jit(solution)/shard_map/cg_fault/pallas_call | solution.py:570
  20.0 0.8 %finish.1 = (f32[3,20,768]{2,1,0:T(8,128)}, f32[3,20,768]{2,1,0:T(8,128)}, f32[10,128]{1,0:T(8,128)}, f32[10,128]{1,0:T(8,128)}) custom-call(f32[3,20,768]{2,1,0:T(8,128)S(1)} %get-tuple-element.8.refs_0_, f32[3,20,768]{2,1,0:T(8,128)S(1)} %get-tuple-element.9.refs_1_, f32[10,128]{1,0:T(8,128)S(1)} %get-tuple-element.10.refs_2_, ...), custom_call_target="tpu_custom_call" | custom-call | tf_op jit(solution)/shard_map/finish/pallas_call | solution.py:608

commit v3 on v2

--- a/solution.py
+++ b/solution.py
@@ -14,7 +14,6 @@
 RATE_DAMP = 0.5
 SHEAR_SOFT = 0.01
 
-HIGHEST = lax.Precision.HIGHEST
 MESH = pl.DeviceIdType.MESH
 F32, BF16 = jnp.float32, jnp.bfloat16
 LANES = 128
@@ -29,8 +28,9 @@
     return lax.broadcasted_iota(jnp.int32, shape, dim)
 
 
-def exact_dot(a, b):
-    return lax.dot(a, b, precision=HIGHEST, preferred_element_type=F32)
+def place(rows, value, cols):
+    moved = lax.dot(rows, value, preferred_element_type=F32).astype(BF16)
+    return lax.dot(moved, cols, preferred_element_type=F32)
 
 
 def split(x):
@@ -181,7 +181,7 @@
             pl.semaphore_signal(barrier, inc=1, device_id=peer(d), device_id_type=MESH)
             return carry
 
-        lax.fori_loop(1, count, greet, 0)
+        lax.fori_loop(1, count, greet, 0, unroll=flat)
 
     wait_first()
 
@@ -189,28 +189,26 @@
     col = iota((20, wide), 1)
     inner = lax.rem(col, FIELD)
     node_of = jnp.where((col < 3 * FIELD) & (inner < 3 * STRIDE), lax.rem(inner, STRIDE), -1)
-    spread = (node_of == iota((20, wide), 0)).astype(F32)
+    spread = (node_of == iota((20, wide), 0)).astype(F32).astype(BF16)
     row = iota((ROWS, 10), 0)
-    lift = ((lax.rem(row, 10) == iota((ROWS, 10), 1)) & (row < 30)).astype(F32)
+    lift = ((lax.rem(row, 10) == iota((ROWS, 10), 1)) & (row < 30)).astype(F32).astype(BF16)
     same = lax.div(iota((ROWS, wide), 0), 10) == lax.div(
         lax.rem(iota((ROWS, wide), 1), FIELD), STRIDE
     )
     third = iota((1, wide), 1) >= 2 * FIELD
 
-    def store_op(at, value):
-        high, low = split(value)
-        ops[pl.ds(at, value.shape[0]), :] = jnp.where(
-            third, low.astype(F32), high.astype(F32)
-        ).astype(BF16)
+    def store_op(at, high, low):
+        ops[pl.ds(at, high.shape[0]), :] = jnp.where(third, low, high).astype(BF16)
 
     faces = []
     for f in range(4):
-        full = exact_dot(exact_dot(lift, face_trace[:, f, :]), spread)
-        faces.append(jnp.where(same, full, 0.0))
-    face_all = jnp.concatenate(faces, axis=0)
-    store_op(0, face_all)
-    back = jnp.transpose(face_all[:, :LANES])[:FIELD]
-    back_high, back_low = split(back)
+        parts = split(face_trace[:, f, :])
+        faces.append([jnp.where(same, place(lift, part, spread), 0.0) for part in parts])
+    face_high, face_low = [jnp.concatenate([face[i] for face in faces], axis=0) for i in range(2)]
+    store_op(0, face_high, face_low)
+    back_high, back_low = [jnp.transpose(x[:, :LANES])[:FIELD] for x in (face_high, face_low)]
+    back = back_high + back_low
+    back_high, back_low = back_high.astype(BF16), back_low.astype(BF16)
     back3[...] = jnp.concatenate([back_high, back_high, back_low], axis=1)
 
     a60 = iota((60, wide), 0)
@@ -218,21 +216,21 @@
     in60 = lax.rem(c60, FIELD)
     place60 = lax.div(in60, STRIDE) * 20 + lax.rem(in60, STRIDE)
     ok60 = (c60 < 3 * FIELD) & (in60 < 3 * STRIDE) & (lax.rem(in60, STRIDE) < 20)
-    right = (ok60 & (place60 == a60)).astype(F32)
+    right = (ok60 & (place60 == a60)).astype(F32).astype(BF16)
     rows60 = iota((FIELD, 60), 0)
     left = (
         (rows60 < 3 * STRIDE)
         & (lax.rem(rows60, STRIDE) < 20)
         & (lax.div(rows60, STRIDE) * 20 + lax.rem(rows60, STRIDE) == iota((FIELD, 60), 1))
-    ).astype(F32)
+    ).astype(F32).astype(BF16)
     eye = iota((FIELD, wide), 0) == iota((FIELD, wide), 1)
     pad_row = iota((FIELD, 1), 0)
     is_pad = (pad_row >= 3 * STRIDE) | (lax.rem(pad_row, STRIDE) >= 20)
     diag = []
     for m in range(2):
-        ref = exact_dot(exact_dot(left, stiffness_ref[:, m, :]), right)
-        store_op(LANES + m * FIELD, ref)
-        entries = jnp.sum(jnp.where(eye, ref, 0.0), axis=1, keepdims=True)
+        high, low = [place(left, part, right) for part in split(stiffness_ref[:, m, :])]
+        store_op(LANES + m * FIELD, high, low)
+        entries = jnp.sum(jnp.where(eye, high + low, 0.0), axis=1, keepdims=True)
         diag.append(jnp.where(is_pad, 1.0, entries))
     squares = back * back
     weights = []
@@ -268,13 +266,13 @@
                 preferred_element_type=F32,
             )
 
-    def pack_groups(ref, phase, at):
+    def pack_traces(phase):
         for f in range(4):
             for k in range(tiles):
-                packed[at, f * tiles + k] = pack(ref[phase, k, f * ROWS : (f + 1) * ROWS, :])
-
-    def local_sources(at):
-        return [lambda g=g: packed[at, g] for g in range(n_groups)]
+                packed[f * tiles + k] = pack(trace[phase, k, f * ROWS : (f + 1) * ROWS, :])
+
+    def local_sources():
+        return [lambda g=g: packed[g] for g in range(n_groups)]
 
     nothing = jnp.zeros((PACKED, LANES), jnp.int32)
 
@@ -307,8 +305,8 @@
             pl.when(condition)(act)
 
     def send_halo(phase, before):
-        pack_groups(trace, phase, 0)
-        sources = local_sources(0)
+        pack_traces(phase)
+        sources = local_sources()
         copies = halo_copies(phase)
         for part in range(n_sub + 1):
             count = gs if part < n_sub - 1 else gv
@@ -342,7 +340,7 @@
         return adjacency[f : f + 1, k * LANES : (k + 1) * LANES]
 
     def near_local():
-        sources = local_sources(0)
+        sources = local_sources()
         for f in range(4):
             for k in range(tiles):
                 near[f * tiles + k] = pick(codes_of(f, k), sources, 0, nothing)
@@ -386,6 +384,35 @@
             total = total + rows[:, k * LANES : (k + 1) * LANES]
         return total
 
+    def pick_weight(codes):
+        group = jnp.broadcast_to(lax.shift_right_arithmetic(codes, 7), (8, LANES))
+        lane = jnp.broadcast_to(jnp.bitwise_and(codes, LANES - 1), (8, LANES))
+        out = jnp.zeros((8, LANES), F32)
+        for g in range(n_groups):
+            f, k = g // tiles, g % tiles
+            block = jnp.broadcast_to(penalty[f : f + 1, k * LANES : (k + 1) * LANES], (8, LANES))
+            taken = jnp.take_along_axis(block, lane, axis=1, mode="promise_in_bounds")
+            out = jnp.where(group == g, taken, out)
+        return out[0:1]
+
+    def fault_part(phase):
+        own = local_sources()
+        others = [lambda g=g: near[g] for g in range(n_groups)]
+        for d in range(n_sub):
+            codes = fault_codes[pl.ds(lax.rem(s + d, n_sub), 1), :]
+            jump = unpack(pick(codes, own, 0, nothing)) - unpack(pick(codes, others, 0, nothing))
+            fault_buf[d, phase] = pick_weight(codes) * jump
+
+    def fault_copy(d):
+        return pltpu.make_async_remote_copy(
+            src_ref=fault_buf.at[d],
+            dst_ref=fault_recv.at[d - 1],
+            send_sem=fault_s.at[d - 1],
+            recv_sem=fault_r.at[d - 1],
+            device_id=sub_peer(d),
+            device_id_type=MESH,
+        )
+
     make_traces(0, 0)
     send_halo(0, lambda: pl.semaphore_wait(barrier, sum(count - 1 for _, count in rounds)))
     near_local()
@@ -403,6 +430,7 @@
     sin_polar = jnp.sin(polar)
     normal = [sin_polar * jnp.cos(azimuth), sin_polar * jnp.sin(azimuth), jnp.cos(polar)]
 
+    fault_part(0)
     wait_halo(0)
     make_flux(0)
     finish_image(0, field, 2)
@@ -419,20 +447,18 @@
     ]
     p_vol, q_vol = dot_tile(field[0], volume[...]), dot_tile(field[3], volume[...])
 
-    def fault_part(phase):
-        pack_groups(flux, phase, 1)
-        sources = local_sources(1)
-        for d in range(n_sub):
-            codes = fault_codes[pl.ds(lax.rem(s + d, n_sub), 1), :]
-            fault_buf[d, phase] = unpack(pick(codes, sources, 0, nothing))
-
-    fault_part(0)
+    fault_part(1)
+    for d in range(1, n_sub):
+        fault_copy(d).start()
     wait_halo(1)
     p_flux, q_flux = make_flux(1)
 
     parts = [*early, p_vol + p_flux, q_vol + q_flux]
     parts = [jnp.sum(x, axis=0, keepdims=True) for x in parts]
     tile = jnp.concatenate([*parts, jnp.zeros((3, LANES), F32)], axis=0)
+    tile = jnp.broadcast_to(jnp.sum(tile, axis=1, keepdims=True), (8, LANES))
+    on_lane = iota((8, LANES), 0) == iota((8, LANES), 1)
+    line = jnp.sum(jnp.where(on_lane, tile, 0.0), axis=0, keepdims=True)
 
     def start_sums(buf, at, peer, count):
         def body(d, carry):
@@ -446,29 +472,16 @@
             ).start()
             return carry
 
-        lax.fori_loop(1, count, body, 0)
+        lax.fori_loop(1, count, body, 0, unroll=flat)
 
     def whole(buf, sem, at, count):
         view = buf.at[pl.ds(1, count - 1)]
         pltpu.make_async_copy(view, view, sem.at[at]).wait()
 
     bufs = [sums, sums_two]
-    sums[0] = tile
+    sums[0] = line
     start_sums(sums, 0, *rounds[0])
 
-    def fault_copy(d):
-        return pltpu.make_async_remote_copy(
-            src_ref=fault_buf.at[d],
-            dst_ref=fault_recv.at[d - 1],
-            send_sem=fault_s.at[d - 1],
-            recv_sem=fault_r.at[d - 1],
-            device_id=sub_peer(d),
-            device_id_type=MESH,
-        )
-
-    fault_part(1)
-    for d in range(1, n_sub):
-        fault_copy(d).start()
     finish_image(1, image, 0)
     wait_sent(0)
     wait_sent(1)
@@ -479,8 +492,7 @@
         if at + 1 < len(rounds):
             bufs[at + 1][0] = total
             start_sums(bufs[at + 1], at + 1, *rounds[at + 1])
-    total = jnp.sum(total, axis=1, keepdims=True)
-    rz, pw, qw, pv, qv = [total[i : i + 1] for i in range(5)]
+    rz, pw, qw, pv, qv = [total[:, i : i + 1] for i in range(5)]
 
     step = rz / pw
     rz_new = step * step * qw - rz
@@ -581,7 +593,7 @@
             pltpu.VMEM((FIELD, 3 * LANES), BF16),
             pltpu.VMEM((FIELD, elems), F32),
             pltpu.VMEM((2, tiles, LANES, LANES), F32),
-            pltpu.VMEM((2, n_groups, PACKED, LANES), jnp.int32),
+            pltpu.VMEM((n_groups, PACKED, LANES), jnp.int32),
             pltpu.VMEM((remote, PACKED, LANES), jnp.int32),
             pltpu.VMEM((n_groups, PACKED, LANES), jnp.int32),
             pltpu.VMEM((2, tiles, LANES, LANES), F32),
@@ -592,8 +604,8 @@
             pltpu.VMEM((8, LANES), jnp.int32),
             pltpu.VMEM((n_sub, 2, ROWS, LANES), F32),
             pltpu.VMEM((max(n_sub - 1, 1), 2, ROWS, LANES), F32),
-            pltpu.VMEM((counts[0], 8, LANES), F32),
-            pltpu.VMEM((counts[1], 8, LANES), F32),
+            pltpu.VMEM((counts[0], 1, LANES), F32),
+            pltpu.VMEM((counts[1], 1, LANES), F32),
             pltpu.VMEM((ROWS, LANES), F32),
             dma((2, n_sub + 1)),
             dma((2, n_sub + 1)),

time: 21 us -> 21.2 us (level)
    pallas_call x1, Pallas kernels: 19.4 us -> 19.6 us  [local(): pl.pallas_call(functools.partial(kernel, sizes), out_shape=tuple((pltpu.V...]
where the time goes in v3:
time: 21.2 us; the launch traced here: 21.1 us
  Pallas kernels  20.4 us (96%)
  between operations  0.64 us (3%)
    pallas_call x1, Pallas kernels, local(): pl.pallas_call(functools.partial(kernel, sizes), out_shape=tuple((pltpu.V...  19.6 us
    pallas_call x1, Pallas kernels, local(): pl.pallas_call(finish, out_shape=shapes, in_specs=[vmem] * 4, out_specs=(...  0.8 us

profile of v3, /device:TPU:0, one launch (start us, length us, event | category | flops | bytes accessed | tf_op | source)
XLA Modules:
  0.0 21.1 jit_solution(16383186780378665592)
XLA Ops:
  0.6 19.6 %cg_fault.1 = (f32[3,20,768]{2,1,0:T(8,128)S(1)}, f32[3,20,768]{2,1,0:T(8,128)S(1)}, f32[10,128]{1,0:T(8,128)S(1)}, f32[10,128]{1,0:T(8,128)S(1)}) custom-call(f32[3,20,768]{2,1,0:T(8,128)} %refs_0_.1, f32[6,128]{1,0:T(8,128)} %bitcast.10, s32[6,128]{1,0:T(8,128)} %bitcast.11, f32[60,2,60]{2,1,0:T(2,128)} %bitcast.8, f32[10,4,20]{2,1,0:T(4,128)} %bitcast.9, ...), custom_call_target="tpu_custom_call" | custom-call | tf_op jit(solution)/shard_map/cg_fault/pallas_call | solution.py:582
  20.3 0.8 %finish.1 = (f32[3,20,768]{2,1,0:T(8,128)}, f32[3,20,768]{2,1,0:T(8,128)}, f32[10,128]{1,0:T(8,128)}, f32[10,128]{1,0:T(8,128)}) custom-call(f32[3,20,768]{2,1,0:T(8,128)S(1)} %get-tuple-element.8.refs_0_, f32[3,20,768]{2,1,0:T(8,128)S(1)} %get-tuple-element.9.refs_1_, f32[10,128]{1,0:T(8,128)S(1)} %get-tuple-element.10.refs_2_, ...), custom_call_target="tpu_custom_call" | custom-call | tf_op jit(solution)/shard_map/finish/pallas_call | solution.py:620
